TPU v7x, 32 devices: a whole 2x2x4 slice. The times are simulated.
32 devices in a mesh: grp: 8 (over y, x, core), sub: 4 (over z).
Axes of the slice: x: 2, y: 2, z: 4, core: 2. Of those that a mesh axis runs over, the one named last changes fastest.
Arguments:
- loads: bfloat16 [8, 4, 16, 1536], P('grp', 'sub'), may hold values from -6 to 6
- boundary_values: float32 [16, 6144], replicated, may hold values from -6 to 6
- dirichlet_ids: int32 [8, 4, 3, 128], P('grp', 'sub'), may hold values from 0 to 6143
- dirichlet_coupling: bfloat16 [8, 4, 3, 512, 128], P('grp', 'sub'), may hold values from -0.5 to 0.5
- local_inverse: bfloat16 [8, 4, 3, 512, 512], P('grp', 'sub'), as said below
- local_schur: bfloat16 [8, 4, 3, 512, 512], P('grp', 'sub')
- corner_coupling: bfloat16 [8, 4, 3, 24, 512], P('grp', 'sub'), may hold values from -0.25 to 0.25
- corner_ids: int32 [8, 4, 3, 24], P('grp', 'sub'), may hold values from 0 to 767
- coarse_inverse: bfloat16 [768, 768], P(('grp', 'sub')), as said below
- row_counts: int32 [8, 4, 6], P('grp', 'sub'), may hold values from 0 to 256, as said below
- slot_of: int32 [8, 4, 1536], P('grp', 'sub'), may hold values from 0 to 1535, each once within a row
Outputs:
- multipliers: float32 [8, 4, 16, 1536], P('grp', 'sub')
- residual: float32 [8, 4, 16, 1536], P('grp', 'sub')
Inputs may be any that keep to these rules, and one draw needn't show every extreme that they name: row_counts[g, s, p] for p < 4 equals row_counts[g, p, s], is 0 for p = s and lies in 1 to 256 otherwise; every device reaches 256 with some peer. Column 4 of device (g, s) equals column 5 of device (g - 1, s), lies in 1 to 256, reaches 256 on some device of every slab boundary, and is 0 in the first slab; column 5 is 0 in the last slab. coarse_inverse is symmetric and positive definite. local_inverse and local_schur are symmetric and positive definite.
All inputs are finite; a program needn't handle non-finite values.
Results may differ from a plain program's by a relative error of at most 0.012.
Values may be sent and summed in bfloat16 or wider, within the bound.
A program may use at most 64 MiB of HBM per device.

v0:
```python
import jax
import jax.numpy as jnp
from jax import lax
from jax.sharding import PartitionSpec as P

IFACE = 512
SUBS_DEV = 3
LOADS = 16
CORNERS = 24
SLAB_ROWS = 256
ITERS = 2


def extended(cells, sides, width):
    for axis, dim in sides:
        count = lax.axis_size(axis)
        ends = count - 1
        head = lax.slice_in_dim(cells, 0, width, axis=dim)
        tail = lax.slice_in_dim(cells, cells.shape[dim] - width, cells.shape[dim], axis=dim)
        cells = jnp.concatenate(
            [
                lax.ppermute(tail, axis, [(i, (i + 1) % count) for i in range(ends)]),
                cells,
                lax.ppermute(head, axis, [((i + 1) % count, i) for i in range(ends)]),
            ],
            axis=dim,
        )
    return cells


def per_device(
    loads,
    boundary_values,
    dirichlet_ids,
    dirichlet_coupling,
    local_inverse,
    local_schur,
    corner_coupling,
    corner_ids,
    coarse_inverse,
    row_counts,
    slot_of,
):
    load_cases = loads[0, 0]
    fixed_ids = dirichlet_ids[0, 0]
    fixed_coupling = dirichlet_coupling[0, 0]
    inverse_blocks = local_inverse[0, 0]
    schur_blocks = local_schur[0, 0]
    coupling = corner_coupling[0, 0]
    corner_index = corner_ids[0, 0].reshape(-1)
    counts = row_counts[0, 0]
    slots = slot_of[0, 0]
    n_sub = lax.axis_size("sub")
    length = slots.shape[0]
    peer_rows = (length - 2 * SLAB_ROWS) // n_sub
    within = n_sub * peer_rows
    coarse_size = coarse_inverse.shape[1]
    positions = jnp.arange(length, dtype=jnp.int32)
    slot_inverse = jnp.zeros(length, jnp.int32).at[slots].set(positions)
    column = jnp.where(
        positions < within, positions // peer_rows, n_sub + (positions - within) // SLAB_ROWS
    )
    offset = jnp.where(positions < within, positions % peer_rows, (positions - within) % SLAB_ROWS)
    canon_live = (offset < counts[column]).astype(jnp.float32)
    live_mask = canon_live[slot_inverse][None, :]
    peer_index = slots[:within].reshape(n_sub, peer_rows)
    slab_index = slots[within:].reshape(2, SLAB_ROWS)
    slab_block = lax.all_to_all(coarse_inverse, "sub", split_axis=1, concat_axis=0, tiled=True)

    def partner(values):
        outgoing = jnp.take(values, peer_index, axis=1)
        incoming = lax.all_to_all(outgoing, "sub", split_axis=1, concat_axis=1, tiled=True).reshape(
            LOADS, within
        )
        slab_part = jnp.take(values, slab_index, axis=1)
        padded = extended(slab_part, (("grp", 1),), 1)
        joined = jnp.concatenate([incoming, padded[:, 0], padded[:, 3]], axis=1)
        return jnp.take(joined, slot_inverse, axis=1)

    def apply_tilde(field_b):
        blocks = field_b.reshape(LOADS, SUBS_DEV, IFACE)
        local_part = jnp.einsum(
            "anm,ram->ran", inverse_blocks, blocks, preferred_element_type=jnp.float32
        )
        corner_terms = jnp.einsum(
            "acm,ram->rac", coupling, blocks, preferred_element_type=jnp.float32
        )
        partial_load = (
            jnp.zeros((LOADS, coarse_size), jnp.float32)
            .at[:, corner_index]
            .add(corner_terms.reshape(LOADS, -1))
        )
        column_load = lax.psum_scatter(partial_load, "sub", scatter_dimension=1, tiled=True)
        column_total = lax.psum(column_load, "grp")
        block_term = jnp.einsum(
            "rj,ij->ri",
            column_total.astype(jnp.bfloat16),
            slab_block,
            preferred_element_type=jnp.float32,
        )
        slab_values = lax.psum(block_term, "sub")
        coarse_values = lax.all_gather(slab_values, "grp", axis=1, tiled=True)
        at_corners = (
            jnp.take(coarse_values, corner_index, axis=1)
            .astype(jnp.bfloat16)
            .reshape(LOADS, SUBS_DEV, CORNERS)
        )
        correction = jnp.einsum(
            "acm,rac->ram", coupling, at_corners, preferred_element_type=jnp.float32
        )
        return (local_part + correction).reshape(LOADS, length)

    def jumps(values):
        return live_mask * (values - partner(values))

    picked = jnp.take(boundary_values, fixed_ids, axis=1).astype(jnp.bfloat16)
    lifted_part = jnp.einsum(
        "and,rad->ran", fixed_coupling, picked, preferred_element_type=jnp.float32
    ).reshape(LOADS, length)
    lifted = live_mask * (load_cases.astype(jnp.float32) - lifted_part)
    jump_field = jumps(apply_tilde(lifted.astype(jnp.bfloat16)))
    multipliers = jnp.zeros_like(jump_field)
    residual = jump_field
    search = jump_field
    inner_before = jnp.ones((LOADS,), jnp.float32)
    for step in range(ITERS):
        smoothed = jnp.einsum(
            "anm,ram->ran",
            schur_blocks,
            residual.astype(jnp.bfloat16).reshape(LOADS, SUBS_DEV, IFACE),
            preferred_element_type=jnp.float32,
        ).reshape(LOADS, length)
        precond = 0.25 * live_mask * (smoothed - partner(smoothed))
        inner_now = lax.psum(jnp.sum(residual * precond, axis=1), ("grp", "sub"))
        if step == 0:
            search = precond
        else:
            search = precond + (inner_now / inner_before)[:, None] * search
        tilde = apply_tilde(search.astype(jnp.bfloat16))
        image = jumps(tilde)
        curvature = lax.psum(jnp.sum(search * image, axis=1), ("grp", "sub"))
        step_size = (inner_now / curvature)[:, None]
        multipliers = multipliers + step_size * search
        residual = residual - step_size * image
        inner_before = inner_now
    return (multipliers[None, None], residual[None, None])


def solution(mesh):
    in_specs = (
        P("grp", "sub", None, None),
        P(),
        P("grp", "sub", None, None),
        P("grp", "sub", None, None, None),
        P("grp", "sub", None, None, None),
        P("grp", "sub", None, None, None),
        P("grp", "sub", None, None, None),
        P("grp", "sub", None, None),
        P(("grp", "sub"), None),
        P("grp", "sub", None),
        P("grp", "sub", None),
    )
    out_specs = (P("grp", "sub", None, None), P("grp", "sub", None, None))
    return jax.shard_map(
        per_device, mesh=mesh, in_specs=in_specs, out_specs=out_specs, check_vma=False
    )
```

profile of v0, /device:TPU:0, one launch (start us, length us, event | category | flops | bytes accessed | tf_op | source)
XLA Modules:
  0.0 514.2 jit_solution(13579813224056020885)
XLA Ops:
  11.0 1.6 fusion.113
  12.5 3.8 fusion.93
  17.1 6.2 %scatter_custom_fusion = s32[1536]{0:T(1024)S(1)} fusion(s32[1536]{0:T(1024)S(1)} %fusion.94, s32[1536]{0:T(1024)S(1)} %iota.10, s32[]{:T(128)} %constant.102.clone.1), kind=kCustom, calls=%fused_computation.172 | custom fusion | bytes 6148 | tf_op jit(solution)/shard_map/scatter | solution.py:59
  23.4 8.4 %gather_fusion = f32[1536]{0:T(1024)S(1)} fusion(f32[1536]{0:T(1024)S(1)} %fusion.90, s32[2048]{0:T(1024)S(1)} %pad_clamp_fusion), kind=kCustom, calls=%fused_computation.18 | custom fusion | bytes 18432 | tf_op jit(solution)/shard_map/gather | solution.py:65
  31.8 1.7 copy.313
  33.5 1.4 gather_fusion.1
  36.6 1.7 scatter_custom_fusion.1
  39.8 6.3 %all-to-all-start = ((bf16[24,4,192]{2,0,1:T(8,128)(2,1)}), bf16[24,4,192]{2,0,1:T(8,128)(2,1)S(1)}, u32[]{:S(2)}, u32[]{:S(2)}) async-start(bf16[24,4,192]{2,0,1:T(8,128)(2,1)} %copy.318), calls=%async_computation.1 | async-start | bytes 98304 | tf_op jit(solution)/shard_map/all_to_all | solution.py:68
  47.8 14.3 %reduce-scatter.4.cloned.1.call-done = f32[16,192]{0,1:T(8,128)} async-done(((f32[16,768]{0,1:T(8,128)}), f32[16,192]{0,1:T(8,128)}) %reduce-scatter.4.cloned.1.call-update) | async-done | bytes 12304 | tf_op jit(solution)/shard_map/reduce_scatter | solution.py:93
  62.1 23.7 %psum.70 = bf16[16,192]{0,1:T(8,128)(2,1)S(1)} all-reduce(f32[16,192]{0,1:T(8,128)} %reduce-scatter.4.cloned.1.call-done), channel_id=1, replica_groups=mesh['grp'=8,'sub'=4] {'grp'}, use_global_device_ids=true, to_apply=%region_3.4 | all-reduce | flops 3072 | bytes 18432 | tf_op jit(solution)/shard_map/psum | solution.py:94
  86.0 9.4 %psum.71 = bf16[16,96]{1,0:T(8,128)(2,1)S(1)} all-reduce(f32[16,96]{1,0:T(8,128)S(1)} %fusion.116), channel_id=1, replica_groups=mesh['grp'=8,'sub'=4] {'sub'}, use_global_device_ids=true, to_apply=%region_4.5 | all-reduce | flops 1536 | bytes 9216 | tf_op jit(solution)/shard_map/psum | solution.py:101
  95.4 8.5 %all-gather = bf16[8,96,16]{1,2,0:T(8,128)(2,1)S(1)} all-gather(bf16[1,96,16]{1,2,0:T(8,128)(2,1)S(1)} %bitcast.323), channel_id=1, replica_groups=mesh['grp'=8,'sub'=4] {'grp'}, dimensions={0}, use_global_device_ids=true | all-gather | bytes 27648 | tf_op jit(solution)/shard_map/all_gather | solution.py:102
  107.0 1.3 collective-permute-start.1
  108.3 3.0 collective-permute-start
  111.4 2.8 gather_fusion.3
  115.0 3.3 all-to-all-start.1
  118.3 5.7 %all-to-all-done.1 = f32[16,4,256]{2,0,1:T(8,128)S(1)} async-done(((f32[16,4,256]{2,0,1:T(8,128)}), f32[16,4,256]{2,0,1:T(8,128)S(1)}, u32[]{:S(2)}, u32[]{:S(2)}) %all-to-all-start.1) | async-done | bytes 65568 | tf_op jit(solution)/shard_map/all_to_all | solution.py:72
  125.3 4.8 gather_fusion.5
  130.1 1.4 copy.329
  133.8 2.8 gather_fusion.7
  136.6 5.1 gather_fusion.6
  142.8 1.3 collective-permute-start.3
  144.1 3.0 collective-permute-start.2
  148.9 3.3 all-to-all-start.2
  152.3 5.7 %all-to-all-done.2 = f32[16,4,256]{2,0,1:T(8,128)S(1)} async-done(((f32[16,4,256]{2,0,1:T(8,128)}), f32[16,4,256]{2,0,1:T(8,128)S(1)}, u32[]{:S(2)}, u32[]{:S(2)}) %all-to-all-start.2) | async-done | bytes 65568 | tf_op jit(solution)/shard_map/all_to_all | solution.py:72
  159.2 4.8 gather_fusion.8
  164.0 2.0 copy.338
  167.3 1.7 scatter_custom_fusion.2
  169.0 19.8 %reduce-scatter.6.cloned.1.call-done = f32[16,192]{0,1:T(8,128)} async-done(((f32[16,768]{0,1:T(8,128)}), f32[16,192]{0,1:T(8,128)}) %reduce-scatter.6.cloned.1.call-update) | async-done | bytes 12304 | tf_op jit(solution)/shard_map/reduce_scatter | solution.py:93
  188.8 24.1 %psum.73 = bf16[16,192]{0,1:T(8,128)(2,1)S(1)} all-reduce(f32[16,192]{0,1:T(8,128)} %reduce-scatter.6.cloned.1.call-done), channel_id=1, replica_groups=mesh['grp'=8,'sub'=4] {'grp'}, use_global_device_ids=true, to_apply=%region_9.14 | all-reduce | flops 3072 | bytes 18432 | tf_op jit(solution)/shard_map/psum | solution.py:94
  213.1 9.3 %psum.74 = bf16[16,96]{1,0:T(8,128)(2,1)S(1)} all-reduce(f32[16,96]{1,0:T(8,128)S(1)} %fusion.115), channel_id=1, replica_groups=mesh['grp'=8,'sub'=4] {'sub'}, use_global_device_ids=true, to_apply=%region_10.15 | all-reduce | flops 1536 | bytes 9216 | tf_op jit(solution)/shard_map/psum | solution.py:101
  222.4 8.2 %all-gather.1 = bf16[8,96,16]{1,2,0:T(8,128)(2,1)S(1)} all-gather(bf16[1,96,16]{1,2,0:T(8,128)(2,1)S(1)} %bitcast.324), channel_id=1, replica_groups=mesh['grp'=8,'sub'=4] {'grp'}, dimensions={0}, use_global_device_ids=true | all-gather | bytes 27648 | tf_op jit(solution)/shard_map/all_gather | solution.py:102
  231.4 1.7 gather_fusion.9
  235.7 2.8 gather_fusion.11
  238.5 5.1 gather_fusion.10
  245.9 1.3 select_bitcast_fusion.2
  247.2 3.3 all-to-all-start.3
  252.4 3.0 collective-permute-start.4
  258.9 4.8 gather_fusion.12
  263.7 1.4 copy.353
  265.1 1.6 multiply_reduce_fusion.2
  266.7 43.5 %all-reduce = (f32[16]{0:T(128)}, f32[16]{0:T(128)}) all-reduce(f32[16]{0:T(128)} %get-tuple-element.17, f32[16]{0:T(128)} %get-tuple-element.16), channel_id=1, replica_groups=mesh['grp'=8,'sub'=4] {'grp','sub'}, use_global_device_ids=true, to_apply=%region_6.11 | all-reduce | flops 32 | bytes 256 | tf_op jit(solution)/shard_map/psum | solution.py:134
  310.8 1.6 fusion.103
  313.3 1.6 gather_fusion.14
  314.9 2.8 gather_fusion.13
  319.6 3.7 all-to-all-start.4
  324.6 3.0 collective-permute-start.6
  327.6 1.4 all-to-all-done.4
  329.3 3.7 gather_fusion.15
  333.0 1.4 copy.362
  334.5 43.5 %psum.76 = f32[16]{0:T(128)S(1)} all-reduce(f32[16]{0:T(128)S(1)} %multiply_reduce_fusion.1), channel_id=1, replica_groups=mesh['grp'=8,'sub'=4] {'grp','sub'}, use_global_device_ids=true, to_apply=%region_14.19 | all-reduce | flops 16 | bytes 128 | tf_op jit(solution)/shard_map/psum | solution.py:134
  379.6 1.7 scatter_custom_fusion.3
  381.3 20.9 %reduce-scatter.8.cloned.1.call-done = f32[16,192]{0,1:T(8,128)} async-done(((f32[16,768]{0,1:T(8,128)}), f32[16,192]{0,1:T(8,128)}) %reduce-scatter.8.cloned.1.call-update) | async-done | bytes 12304 | tf_op jit(solution)/shard_map/reduce_scatter | solution.py:93
  402.2 24.2 %psum.77 = bf16[16,192]{0,1:T(8,128)(2,1)S(1)} all-reduce(f32[16,192]{0,1:T(8,128)} %reduce-scatter.8.cloned.1.call-done), channel_id=1, replica_groups=mesh['grp'=8,'sub'=4] {'grp'}, use_global_device_ids=true, to_apply=%region_17.22 | all-reduce | flops 3072 | bytes 18432 | tf_op jit(solution)/shard_map/psum | solution.py:94
  426.5 8.8 %psum.78 = bf16[16,96]{1,0:T(8,128)(2,1)S(1)} all-reduce(f32[16,96]{1,0:T(8,128)S(1)} %fusion.114), channel_id=1, replica_groups=mesh['grp'=8,'sub'=4] {'sub'}, use_global_device_ids=true, to_apply=%region_18.23 | all-reduce | flops 1536 | bytes 9216 | tf_op jit(solution)/shard_map/psum | solution.py:101
  435.4 8.6 %all-gather.2 = bf16[8,96,16]{1,2,0:T(8,128)(2,1)S(1)} all-gather(bf16[1,96,16]{1,2,0:T(8,128)(2,1)S(1)} %bitcast.325), channel_id=1, replica_groups=mesh['grp'=8,'sub'=4] {'grp'}, dimensions={0}, use_global_device_ids=true | all-gather | bytes 27648 | tf_op jit(solution)/shard_map/all_gather | solution.py:102
  447.0 2.8 gather_fusion.17
  450.8 3.3 all-to-all-start.5
  454.1 1.3 collective-permute-start.9
  455.4 3.0 collective-permute-start.8
  458.4 1.4 all-to-all-done.5
  460.1 2.6 gather_fusion.19
  464.0 42.0 %psum.79 = f32[16]{0:T(128)S(1)} all-reduce(f32[16]{0:T(128)S(1)} %multiply_reduce_fusion), channel_id=1, replica_groups=mesh['grp'=8,'sub'=4] {'grp','sub'}, use_global_device_ids=true, to_apply=%region_20.25 | all-reduce | flops 16 | bytes 128 | tf_op jit(solution)/shard_map/psum | solution.py:141
  506.0 1.7 subtract_bitcast_fusion
  (186 shorter events, 45.7 us)
Async XLA Ops:
  7.2 97.9 %copy-start = (bf16[1,1,3,512,512]{4,3,2,1,0:T(8,128)(2,1)S(1)}, bf16[1,1,3,512,512]{4,3,2,1,0:T(8,128)(2,1)}, u32[]{:S(2)}) copy-start(bf16[1,1,3,512,512]{4,3,2,1,0:T(8,128)(2,1)} %param.23) | copy-start | bytes 4718596
  7.2 55.0 %reduce-scatter.4.cloned.1.call-start = ((), (), s32[]{:S(2)}) async-start(), calls=%async_computation.9 | async-start | bytes 491520 | tf_op jit(solution)/shard_map/reduce_scatter | solution.py:93
  31.7 4.6 copy-start.2
  39.8 46.0 %all-to-all-start = ((bf16[24,4,192]{2,0,1:T(8,128)(2,1)}), bf16[24,4,192]{2,0,1:T(8,128)(2,1)S(1)}, u32[]{:S(2)}, u32[]{:S(2)}) async-start(bf16[24,4,192]{2,0,1:T(8,128)(2,1)} %copy.318), calls=%async_computation.1 | async-start | bytes 98304 | tf_op jit(solution)/shard_map/all_to_all | solution.py:68
  46.2 59.3 %copy-start.13 = (pred[72]{0:T(512)(128)(4,1)}, pred[72]{0:T(512)(128)(4,1)S(1)}, u32[]{:S(2)}) copy-start(pred[72]{0:T(512)(128)(4,1)S(1)} %compare_and_fusion.3) | copy-start | bytes 220
  47.7 66.6 %copy-start.6 = (pred[4,256]{1,0:T(4,128)(4,1)}, pred[4,256]{1,0:T(4,128)(4,1)S(1)}, u32[]{:S(2)}) copy-start(pred[4,256]{1,0:T(4,128)(4,1)S(1)} %compare_and_fusion.2) | copy-start | bytes 3076
  47.8 57.8 %copy-start.12 = (s32[1024]{0:T(1024)}, s32[1024]{0:T(1024)S(1)}, u32[]{:S(2)}) copy-start(s32[1024]{0:T(1024)S(1)} %pad_clamp_fusion.2) | copy-start | bytes 12292
  85.9 127.1 %copy-start.4 = (bf16[24,4,192]{2,0,1:T(8,128)(2,1)}, bf16[24,4,192]{2,0,1:T(8,128)(2,1)S(1)}, u32[]{:S(2)}) copy-start(bf16[24,4,192]{2,0,1:T(8,128)(2,1)S(1)} %all-to-all-done) | copy-start | bytes 110596
  107.0 17.0 %collective-permute-start.1 = (f32[16,1,256]{2,0,1:T(8,128)S(1)}, f32[16,1,256]{2,0,1:T(8,128)S(1)}, u32[]{:S(2)}, u32[]{:S(2)}) collective-permute-start(f32[16,1,256]{2,0,1:T(8,128)S(1)} %get-tuple-element.37), channel_id=1, source_target_pairs={{4,0},{8,4},{12,8},{16,12},{20,16},{24,20},{28,24},{5,1},{9,5},{13... | collective-permute-start | bytes 49160 | tf_op jit(solution)/shard_map/ppermute | solution.py:24
  108.3 15.7 %collective-permute-start = (f32[16,1,256]{2,0,1:T(8,128)S(1)}, f32[16,1,256]{2,0,1:T(8,128)S(1)}, u32[]{:S(2)}, u32[]{:S(2)}) collective-permute-start(f32[16,1,256]{2,0,1:T(8,128)S(1)} %get-tuple-element.36), channel_id=1, source_target_pairs={{0,4},{4,8},{8,12},{12,16},{16,20},{20,24},{24,28},{1,5},{5,9},{9,... | collective-permute-start | bytes 49160 | tf_op jit(solution)/shard_map/ppermute | solution.py:22
  115.0 9.0 %all-to-all-start.1 = ((f32[16,4,256]{2,0,1:T(8,128)}), f32[16,4,256]{2,0,1:T(8,128)S(1)}, u32[]{:S(2)}, u32[]{:S(2)}) async-start(f32[16,4,256]{2,0,1:T(8,128)} %select_bitcast_fusion.4), calls=%async_computation.2 | async-start | bytes 131072 | tf_op jit(solution)/shard_map/all_to_all | solution.py:72
  124.1 8.0 %copy-start.1 = (bf16[1,1,3,512,512]{4,3,2,1,0:T(8,128)(2,1)S(1)}, bf16[1,1,3,512,512]{4,3,2,1,0:T(8,128)(2,1)}, u32[]{:S(2)}) copy-start(bf16[1,1,3,512,512]{4,3,2,1,0:T(8,128)(2,1)} %param.24) | copy-start | bytes 4718596
  132.6 15.7 %copy-start.7 = (pred[4,256]{1,0:T(4,128)(4,1)S(1)}, pred[4,256]{1,0:T(4,128)(4,1)}, u32[]{:S(2)}) copy-start(pred[4,256]{1,0:T(4,128)(4,1)} %copy-done.6) | copy-start | bytes 3076
  142.8 15.3 %collective-permute-start.3 = (f32[16,1,256]{2,0,1:T(8,128)S(1)}, f32[16,1,256]{2,0,1:T(8,128)S(1)}, u32[]{:S(2)}, u32[]{:S(2)}) collective-permute-start(f32[16,1,256]{2,0,1:T(8,128)S(1)} %get-tuple-element.35), channel_id=1, source_target_pairs={{4,0},{8,4},{12,8},{16,12},{20,16},{24,20},{28,24},{5,1},{9,5},{13... | collective-permute-start | bytes 49160 | tf_op jit(solution)/shard_map/ppermute | solution.py:24
  144.1 14.0 %collective-permute-start.2 = (f32[16,1,256]{2,0,1:T(8,128)S(1)}, f32[16,1,256]{2,0,1:T(8,128)S(1)}, u32[]{:S(2)}, u32[]{:S(2)}) collective-permute-start(f32[16,1,256]{2,0,1:T(8,128)S(1)} %get-tuple-element.34), channel_id=1, source_target_pairs={{0,4},{4,8},{8,12},{12,16},{16,20},{20,24},{24,28},{1,5},{5,9},{9,... | collective-permute-start | bytes 49160 | tf_op jit(solution)/shard_map/ppermute | solution.py:22
  148.9 9.1 %all-to-all-start.2 = ((f32[16,4,256]{2,0,1:T(8,128)}), f32[16,4,256]{2,0,1:T(8,128)S(1)}, u32[]{:S(2)}, u32[]{:S(2)}) async-start(f32[16,4,256]{2,0,1:T(8,128)} %select_bitcast_fusion.3), calls=%async_computation.3 | async-start | bytes 131072 | tf_op jit(solution)/shard_map/all_to_all | solution.py:72
  152.2 36.6 %reduce-scatter.6.cloned.1.call-start = ((), (), s32[]{:S(2)}) async-start(), calls=%async_computation.10 | async-start | bytes 491520 | tf_op jit(solution)/shard_map/reduce_scatter | solution.py:93
  247.2 9.0 %all-to-all-start.3 = ((f32[16,4,256]{2,0,1:T(8,128)}), f32[16,4,256]{2,0,1:T(8,128)S(1)}, u32[]{:S(2)}, u32[]{:S(2)}) async-start(f32[16,4,256]{2,0,1:T(8,128)} %select_bitcast_fusion.2), calls=%async_computation.5 | async-start | bytes 131072 | tf_op jit(solution)/shard_map/all_to_all | solution.py:72
  251.1 5.1 collective-permute-start.5
  252.4 4.1 collective-permute-start.4
  256.2 0.6 copy-start.10
  256.4 0.6 copy-start.11
  310.8 1.6 copy-start.15
  313.0 6.0 %copy-start.8 = (pred[4,256]{1,0:T(4,128)(4,1)S(1)}, pred[4,256]{1,0:T(4,128)(4,1)}, u32[]{:S(2)}) copy-start(pred[4,256]{1,0:T(4,128)(4,1)} %copy-done.6) | copy-start | bytes 3076
  319.6 14.8 %copy-start.3 = (f32[16,1536]{1,0:T(8,128)S(1)}, f32[16,1536]{1,0:T(8,128)}, u32[]{:S(2)}) copy-start(f32[16,1536]{1,0:T(8,128)} %get-tuple-element.23) | copy-start | bytes 294916
  319.6 9.4 %all-to-all-start.4 = ((f32[16,4,256]{2,0,1:T(8,128)}), f32[16,4,256]{2,0,1:T(8,128)S(1)}, u32[]{:S(2)}, u32[]{:S(2)}) async-start(f32[16,4,256]{2,0,1:T(8,128)} %select_bitcast_fusion.1), calls=%async_computation.6 | async-start | bytes 131072 | tf_op jit(solution)/shard_map/all_to_all | solution.py:72
  323.3 78.9 %reduce-scatter.8.cloned.1.call-start = ((), (), s32[]{:S(2)}) async-start(), calls=%async_computation.11 | async-start | bytes 491520 | tf_op jit(solution)/shard_map/reduce_scatter | solution.py:93
  323.3 5.7 %collective-permute-start.7 = (f32[16,1,256]{2,0,1:T(8,128)S(1)}, f32[16,1,256]{2,0,1:T(8,128)S(1)}, u32[]{:S(2)}, u32[]{:S(2)}) collective-permute-start(f32[16,1,256]{2,0,1:T(8,128)S(1)} %get-tuple-element.31), channel_id=1, source_target_pairs={{4,0},{8,4},{12,8},{16,12},{20,16},{24,20},{28,24},{5,1},{9,5},{13... | collective-permute-start | bytes 49160 | tf_op jit(solution)/shard_map/ppermute | solution.py:24
  324.6 4.5 collective-permute-start.6
  329.0 49.5 %copy-start.19 = (f32[16]{0:T(128)S(1)}, f32[16]{0:T(128)}, u32[]{:S(2)}) copy-start(f32[16]{0:T(128)} %get-tuple-element.18) | copy-start | bytes 196
  333.0 93.4 %copy-start.5 = (bf16[24,4,192]{2,0,1:T(8,128)(2,1)S(1)}, bf16[24,4,192]{2,0,1:T(8,128)(2,1)}, u32[]{:S(2)}) copy-start(bf16[24,4,192]{2,0,1:T(8,128)(2,1)} %copy-done.4) | copy-start | bytes 110596
  333.0 111.9 %copy-start.14 = (pred[72]{0:T(512)(128)(4,1)S(1)}, pred[72]{0:T(512)(128)(4,1)}, u32[]{:S(2)}) copy-start(pred[72]{0:T(512)(128)(4,1)} %copy-done.13) | copy-start | bytes 220
  378.0 0.5 copy-start.17
  445.7 4.4 copy-start.9
  450.8 9.0 %all-to-all-start.5 = ((f32[16,4,256]{2,0,1:T(8,128)}), f32[16,4,256]{2,0,1:T(8,128)S(1)}, u32[]{:S(2)}, u32[]{:S(2)}) async-start(f32[16,4,256]{2,0,1:T(8,128)} %select_bitcast_fusion), calls=%async_computation.8 | async-start | bytes 131072 | tf_op jit(solution)/shard_map/all_to_all | solution.py:72
  454.1 5.7 %collective-permute-start.9 = (f32[16,1,256]{2,0,1:T(8,128)S(1)}, f32[16,1,256]{2,0,1:T(8,128)S(1)}, u32[]{:S(2)}, u32[]{:S(2)}) collective-permute-start(f32[16,1,256]{2,0,1:T(8,128)S(1)} %get-tuple-element.29), channel_id=1, source_target_pairs={{4,0},{8,4},{12,8},{16,12},{20,16},{24,20},{28,24},{5,1},{9,5},{13... | collective-permute-start | bytes 49160 | tf_op jit(solution)/shard_map/ppermute | solution.py:24
  455.4 4.4 collective-permute-start.8
  459.8 46.2 %copy-start.18 = (f32[16]{0:T(128)S(1)}, f32[16]{0:T(128)}, u32[]{:S(2)}) copy-start(f32[16]{0:T(128)} %copy-done.17) | copy-start | bytes 196
  459.8 46.2 %copy-start.16 = (f32[16]{0:T(128)S(1)}, f32[16]{0:T(128)}, u32[]{:S(2)}) copy-start(f32[16]{0:T(128)} %copy-done.15) | copy-start | bytes 196
Sparse Core Ops, SparseCore 0:
  38.4 23.6 reduce-scatter.3
  169.1 19.6 reduce-scatter.5
  381.4 20.7 reduce-scatter.7
where the time goes:
time: 517 us; the launch traced here: 514 us
  blocking collectives  254 us (49%)
  local copies, waits for them, and re-layouts  98.3 us (19%)
  waiting for transfers between devices  70.4 us (14%)
  starting transfers between devices  44.8 us (9%)
  other arithmetic  27.1 us (5%)
  between operations  14.6 us (3%)
  matrix products  5.2 us (1%)
    psum x2, blocking collectives, per_device(): inner_now = lax.psum(jnp.sum(residual * precond, axis=1), ('grp', 'sub'))  87 us
    psum x3, blocking collectives, apply_tilde(): column_total = lax.psum(column_load, 'grp')  72 us
    reduce_scatter x3, waiting for transfers between devices, apply_tilde(): lax.psum_scatter(partial_load, 'sub', scatter_dimension=1, tiled=True)  55.1 us
    psum x1, blocking collectives, per_device(): curvature = lax.psum(jnp.sum(search * image, axis=1), ('grp', 'sub'))  42 us
    psum x3, blocking collectives, apply_tilde(): slab_values = lax.psum(block_term, 'sub')  27.5 us
    gather x10, local copies, waits for them, and re-layouts, partner(): return jnp.take(joined, slot_inverse, axis=1)  27 us
    all_gather x3, blocking collectives, apply_tilde(): coarse_values = lax.all_gather(slab_values, 'grp', axis=1, tiled=True)  25.3 us
    gather x10, local copies, waits for them, and re-layouts, partner(): outgoing = jnp.take(values, peer_index, axis=1)  21.6 us
  transfers between devices with their start and end apart: 19, of which 9 were waited for; matrix products, arithmetic and copies ran while one was open for 2% of the time, Pallas kernels for 0%

commit v1 on v0

--- a/solution.py
+++ b/solution.py
@@ -1,7 +1,10 @@
 import jax
 import jax.numpy as jnp
 from jax import lax
+from jax.experimental import pallas as pl
+from jax.experimental.pallas import tpu as pltpu
 from jax.sharding import PartitionSpec as P
+import functools
 
 IFACE = 512
 SUBS_DEV = 3
@@ -9,6 +12,8 @@
 CORNERS = 24
 SLAB_ROWS = 256
 ITERS = 2
+LANES = 128
+WHOLE_COARSE_BYTES = 4 << 20
 
 
 def extended(cells, sides, width):
@@ -28,7 +33,7 @@
     return cells
 
 
-def per_device(
+def spread_device(
     loads,
     boundary_values,
     dirichlet_ids,
@@ -146,6 +151,309 @@
     return (multipliers[None, None], residual[None, None])
 
 
+F32 = jnp.float32
+BF16 = jnp.bfloat16
+MESH = pl.DeviceIdType.MESH
+NT = (((1,), (1,)), ((), ()))
+
+
+def mm(a, b):
+    return jnp.dot(a, b, preferred_element_type=F32)
+
+
+def mm_nt(a, b):
+    return lax.dot_general(a, b, NT, preferred_element_type=F32)
+
+
+def onehot(ids_row, first, rows):
+    place = lax.broadcasted_iota(jnp.int32, (rows, ids_row.shape[1]), 0) + first
+    return jnp.where(place == ids_row, 1.0, 0.0).astype(BF16)
+
+
+def fused_kernel(
+    n_grp, n_sub, peer_rows, coarse,
+    loads_ref, bound_ref, fixed_ref, fixcpl_ref, inv_ref, schur_ref, cpl_ref, target_ref, cinv_ref,
+    counts_ref, slots_ref,
+    mult_ref, res_ref,
+    perm, cplf, cplb, cinvf, cinvb, place, ids_all, cinv_all, to_peer, from_peer, to_slab, from_slab,
+    slab_terms, slab_loads,
+    id_send, id_recv, cz_send, cz_recv, cg_send, cg_recv,
+    p_send, p_recv, h_send, h_recv, t_send, t_recv, l_send, l_recv,
+):
+    g = lax.axis_index("grp")
+    s = lax.axis_index("sub")
+    length = slots_ref.shape[1]
+    within = n_sub * peer_rows
+    corners = SUBS_DEV * CORNERS
+    own_rows = coarse // (n_grp * n_sub)
+
+    ids_all[s] = target_ref[...]
+    cinv_all[g, s] = cinv_ref[...]
+    from_peer[...] = jnp.zeros_like(from_peer)
+    from_slab[...] = jnp.zeros_like(from_slab)
+
+    barrier = pltpu.get_barrier_semaphore()
+    for k in range(1, n_sub):
+        pl.semaphore_signal(barrier, inc=1, device_id=(g, lax.rem(s + k, n_sub)), device_id_type=MESH)
+    for k in range(1, n_grp):
+        pl.semaphore_signal(barrier, inc=1, device_id=(lax.rem(g + k, n_grp), s), device_id_type=MESH)
+    pl.semaphore_wait(barrier, n_sub + n_grp - 2)
+
+    def over_sub(buf_at, send, recv):
+        copies = []
+        for k in range(1, n_sub):
+            copies.append(pltpu.make_async_remote_copy(
+                src_ref=buf_at, dst_ref=buf_at, send_sem=send.at[k], recv_sem=recv.at[k],
+                device_id=(g, lax.rem(s + k, n_sub)), device_id_type=MESH))
+        for copy in copies:
+            copy.start()
+        return copies
+
+    def over_grp(buf_at, send, recv):
+        copies = []
+        for k in range(1, n_grp):
+            copies.append(pltpu.make_async_remote_copy(
+                src_ref=buf_at, dst_ref=buf_at, send_sem=send.at[k], recv_sem=recv.at[k],
+                device_id=(lax.rem(g + k, n_grp), s), device_id_type=MESH))
+        for copy in copies:
+            copy.start()
+        return copies
+
+    id_copies = over_sub(ids_all.at[s], id_send, id_recv)
+    cz_copies = over_sub(cinv_all.at[g, s], cz_send, cz_recv)
+
+    chunk = 128
+
+    @pl.loop(0, length // chunk)
+    def _(i):
+        start = pl.multiple_of(i * chunk, chunk)
+        perm[pl.ds(start, chunk), :] = onehot(slots_ref[...], start, chunk)
+
+    column = lax.broadcasted_iota(jnp.int32, (LOADS, length), 1)
+    low = jnp.zeros((LOADS, length), jnp.int32)
+    count = jnp.zeros((LOADS, length), jnp.int32)
+    for p in range(n_sub + 2):
+        first = p * peer_rows if p <= n_sub else within + SLAB_ROWS
+        low = jnp.where(column >= first, first, low)
+        count = jnp.where(column >= first, counts_ref[p], count)
+    canon_live = jnp.where(column - low < count, 1.0, 0.0).astype(BF16)
+    live = mm_nt(canon_live, perm[...])
+
+    cplf[...] = jnp.zeros_like(cplf)
+    for a in range(SUBS_DEV):
+        cplf[a * CORNERS:(a + 1) * CORNERS, a * IFACE:(a + 1) * IFACE] = cpl_ref[a].astype(F32)
+    cplb[...] = cplf[...].astype(BF16)
+
+    bound = bound_ref[...].astype(BF16)
+    lifts = []
+    for a in range(SUBS_DEV):
+        picked = mm(bound, onehot(fixed_ref[a:a + 1, :], 0, bound_ref.shape[1]))
+        lifts.append(mm_nt(picked.astype(BF16), fixcpl_ref[a]))
+    lifted = live * (loads_ref[...].astype(F32) - jnp.concatenate(lifts, axis=1))
+
+    for copy in cz_copies:
+        copy.wait()
+    cg_copies = over_grp(cinv_all.at[g], cg_send, cg_recv)
+    for copy in id_copies:
+        copy.wait()
+    for q in range(n_sub):
+        place[:, q * LANES:(q + 1) * LANES] = onehot(ids_all[q], 0, coarse + LANES)
+    own_place = onehot(target_ref[...], 0, coarse)
+
+    def blocks_apply(ref, field_b):
+        return jnp.concatenate(
+            [mm(field_b[:, a * IFACE:(a + 1) * IFACE], ref[a]) for a in range(SUBS_DEV)], axis=1)
+
+    lane = lax.broadcasted_iota(jnp.int32, (LOADS, LANES), 1)
+
+    def row_sum(x):
+        return jnp.sum(x, axis=1, keepdims=True)
+
+    def tilde(i, field, extra):
+        field_b = field.astype(BF16)
+        message = mm_nt(field_b, cplb[...])
+        local = blocks_apply(inv_ref, field_b)
+        sums = extra(local)
+        for k, part in enumerate(sums):
+            message = jnp.where(lane == corners + k, part, message)
+        slab_terms[i, s] = message
+        for copy in over_sub(slab_terms.at[i, s], t_send.at[i], t_recv.at[i]):
+            copy.wait()
+        terms = jnp.concatenate([slab_terms[i, q] for q in range(n_sub)], axis=1)
+        high = terms.astype(BF16)
+        rest = (terms - high.astype(F32)).astype(BF16)
+        both = mm_nt(jnp.concatenate([high, rest], axis=0), place[...])
+        dense = both[:LOADS] + both[LOADS:]
+        total = dense[:, coarse:]
+        total_high = total.astype(BF16)
+        slab_loads[i, g] = jnp.concatenate(
+            [dense[:, :coarse].astype(BF16), total_high, (total - total_high.astype(F32)).astype(BF16)], axis=1)
+        for copy in over_grp(slab_loads.at[i, g], l_send.at[i], l_recv.at[i]):
+            copy.wait()
+        if i == 0:
+            for copy in cg_copies:
+                copy.wait()
+            for d in range(n_grp * n_sub):
+                part = cinv_all[d // n_sub, d % n_sub].astype(F32)
+                cinvf[d * own_rows:(d + 1) * own_rows, :] = part[:own_rows]
+            cinvb[...] = cinvf[...].astype(BF16)
+        whole = slab_loads[i, 0].astype(F32)
+        for q in range(1, n_grp):
+            whole = whole + slab_loads[i, q].astype(F32)
+        load = whole[:, :coarse]
+        values = mm(load.astype(BF16), cinvb[...])
+        corner_values = mm(values.astype(BF16), own_place)
+        result = local + mm(corner_values.astype(BF16), cplb[...])
+        scalars = whole[:, coarse:coarse + LANES] + whole[:, coarse + LANES:]
+        found = [row_sum(jnp.where(lane == k, scalars, 0.0)) for k in range(len(sums))]
+        return result, local, load, values, found
+
+    def partner(i, field):
+        out = mm(field.astype(BF16), perm[...]).astype(BF16)
+        for q in range(n_sub):
+            to_peer[i, q] = out[:, q * peer_rows:(q + 1) * peer_rows]
+        for q in range(2):
+            to_slab[i, q] = out[:, within + q * SLAB_ROWS:within + (q + 1) * SLAB_ROWS]
+        down = pltpu.make_async_remote_copy(
+            src_ref=to_slab.at[i, 0], dst_ref=from_slab.at[i, 1], send_sem=h_send.at[i, 0],
+            recv_sem=h_recv.at[i, 1], device_id=(jnp.maximum(g - 1, 0), s), device_id_type=MESH)
+        up = pltpu.make_async_remote_copy(
+            src_ref=to_slab.at[i, 1], dst_ref=from_slab.at[i, 0], send_sem=h_send.at[i, 1],
+            recv_sem=h_recv.at[i, 0], device_id=(jnp.minimum(g + 1, n_grp - 1), s), device_id_type=MESH)
+
+        @pl.when(g > 0)
+        def _():
+            down.start()
+
+        @pl.when(g < n_grp - 1)
+        def _():
+            up.start()
+
+        copies = []
+        for k in range(1, n_sub):
+            to = lax.rem(s + k, n_sub)
+            copies.append(pltpu.make_async_remote_copy(
+                src_ref=to_peer.at[i, to], dst_ref=from_peer.at[i, s], send_sem=p_send.at[i, k],
+                recv_sem=p_recv.at[i, k], device_id=(g, to), device_id_type=MESH))
+        for copy in copies:
+            copy.start()
+        for copy in copies:
+            copy.wait()
+
+        @pl.when(g > 0)
+        def _():
+            down.wait_send()
+            up.wait_recv()
+
+        @pl.when(g < n_grp - 1)
+        def _():
+            up.wait_send()
+            down.wait_recv()
+
+        joined = jnp.concatenate(
+            [from_peer[i, q] for q in range(n_sub)] + [from_slab[i, q] for q in range(2)], axis=1)
+        return mm_nt(joined, perm[...])
+
+    def smoothed(residual):
+        return blocks_apply(schur_ref, residual.astype(BF16))
+
+    image = tilde(0, lifted, lambda local: [])[0]
+    residual = live * (image - partner(0, image))
+
+    smooth = smoothed(residual)
+    inner_part = 0.5 * row_sum(residual * smooth)
+    first = 0.25 * live * (smooth - partner(1, smooth))
+    image0, local0, load0, values0, (inner0, energy0) = tilde(
+        1, first, lambda local: [inner_part, row_sum(first * local)])
+    energy0 = energy0 + row_sum(load0 * values0)
+    size0 = inner0 / (2.0 * energy0)
+    residual = residual - size0 * (live * (image0 - partner(2, image0)))
+
+    smooth = smoothed(residual)
+    inner_part1 = 0.5 * row_sum(residual * smooth)
+    second = 0.25 * live * (smooth - partner(3, smooth))
+    image1, _, load1, values1, (inner1, energy1, cross) = tilde(
+        2, second, lambda local: [inner_part1, row_sum(second * local), row_sum(second * local0)])
+    ratio = inner1 / inner0
+    energy1 = energy1 + row_sum(load1 * values1)
+    cross = cross + row_sum(load1 * values0)
+    energy = energy1 + ratio * (2.0 * cross + ratio * energy0)
+    size1 = inner1 / (2.0 * energy)
+    search = second + ratio * first
+    image = image1 + ratio * image0
+    mult_ref[...] = size0 * first + size1 * search
+    res_ref[...] = residual - size1 * (live * (image - partner(4, image)))
+
+
+def fused_device(
+    loads,
+    boundary_values,
+    dirichlet_ids,
+    dirichlet_coupling,
+    local_inverse,
+    local_schur,
+    corner_coupling,
+    corner_ids,
+    coarse_inverse,
+    row_counts,
+    slot_of,
+):
+    n_grp, n_sub = lax.axis_size("grp"), lax.axis_size("sub")
+    length = slot_of.shape[2]
+    peer_rows = (length - 2 * SLAB_ROWS) // n_sub
+    coarse = coarse_inverse.shape[1]
+    corners = SUBS_DEV * CORNERS
+    target = jnp.concatenate(
+        [corner_ids[0, 0].reshape(1, corners), coarse + jnp.arange(LANES - corners, dtype=jnp.int32)[None]], axis=1)
+    rows = coarse_inverse.shape[0]
+    held = -(-rows // 16) * 16
+    coarse_rows = jnp.pad(coarse_inverse, ((0, held - rows), (0, 0)))
+    vmem = pl.BlockSpec(memory_space=pltpu.VMEM)
+    smem = pl.BlockSpec(memory_space=pltpu.SMEM)
+    swaps, solves = 2 * ITERS + 1, ITERS + 1
+    dma = pltpu.SemaphoreType.DMA
+    field = jax.ShapeDtypeStruct((LOADS, length), F32)
+    mult, res = pl.pallas_call(
+        functools.partial(fused_kernel, n_grp, n_sub, peer_rows, coarse),
+        out_shape=(field, field),
+        in_specs=[vmem] * 9 + [smem, vmem],
+        out_specs=(vmem, vmem),
+        scratch_shapes=[
+            pltpu.VMEM((length, length), BF16),
+            pltpu.VMEM((LANES, length), F32),
+            pltpu.VMEM((LANES, length), BF16),
+            pltpu.VMEM((coarse, coarse), F32),
+            pltpu.VMEM((coarse, coarse), BF16),
+            pltpu.VMEM((coarse + LANES, n_sub * LANES), BF16),
+            pltpu.VMEM((n_sub, 1, LANES), jnp.int32),
+            pltpu.VMEM((n_grp, n_sub, held, coarse), BF16),
+            pltpu.VMEM((swaps, n_sub, LOADS, peer_rows), BF16),
+            pltpu.VMEM((swaps, n_sub, LOADS, peer_rows), BF16),
+            pltpu.VMEM((swaps, 2, LOADS, SLAB_ROWS), BF16),
+            pltpu.VMEM((swaps, 2, LOADS, SLAB_ROWS), BF16),
+            pltpu.VMEM((solves, n_sub, LOADS, LANES), F32),
+            pltpu.VMEM((solves, n_grp, LOADS, coarse + 2 * LANES), BF16),
+            dma((n_sub,)), dma((n_sub,)), dma((n_sub,)), dma((n_sub,)), dma((n_grp,)), dma((n_grp,)),
+            dma((swaps, n_sub)), dma((swaps, n_sub)), dma((swaps, 2)), dma((swaps, 2)),
+            dma((solves, n_sub)), dma((solves, n_sub)), dma((solves, n_grp)), dma((solves, n_grp)),
+        ],
+        compiler_params=pltpu.CompilerParams(
+            collective_id=0, has_side_effects=True, vmem_limit_bytes=48 << 20),
+    )(
+        loads[0, 0], boundary_values, dirichlet_ids[0, 0], dirichlet_coupling[0, 0], local_inverse[0, 0],
+        local_schur[0, 0], corner_coupling[0, 0], target, coarse_rows, row_counts[0, 0], slot_of[0],
+    )
+    return (mult[None, None], res[None, None])
+
+
+def per_device(*args):
+    coarse = args[8].shape[1]
+    peer_rows = (args[10].shape[2] - 2 * SLAB_ROWS) // lax.axis_size("sub")
+    small = coarse * coarse * args[8].dtype.itemsize <= WHOLE_COARSE_BYTES
+    aligned = peer_rows % LANES == 0 and coarse % LANES == 0 and args[8].shape[0] % 8 == 0
+    return (fused_device if small and aligned else spread_device)(*args)
+
+
 def solution(mesh):
     in_specs = (
         P("grp", "sub", None, None),

time: 517 us -> 93 us (0.18)
  blocking collectives: 254 us -> 0 us
  local copies, waits for them, and re-layouts: 98.3 us -> 10.7 us
  Pallas kernels: 0 us -> 80.4 us
  waiting for transfers between devices: 70.4 us -> 0 us
  starting transfers between devices: 44.8 us -> 0 us
  other arithmetic: 27.1 us -> 0.78 us
  between operations: 14.6 us -> 0.65 us
  matrix products: 5.2 us -> 0 us
    psum x9 -> x0, blocking collectives: 228 us -> none  [the longest x2 87 us: per_device(): inner_now = lax.psum(jnp.sum(residual * precond, axis=1), ('grp', 'sub'))]
    pallas_call x0 -> x1, Pallas kernels: none -> 80.4 us  [fused_device(): pl.pallas_call(functools.partial(fused_kernel, n_grp, n_sub, peer_rows, c...]
    gather x37 -> x0, local copies, waits for them, and re-layouts: 75.7 us -> none  [the longest x10 27 us: partner(): return jnp.take(joined, slot_inverse, axis=1)]
    reduce_scatter x3 -> x0, waiting for transfers between devices: 55.1 us -> none  [apply_tilde(): lax.psum_scatter(partial_load, 'sub', scatter_dimension=1, tiled=True)]
    all_gather x3 -> x0, blocking collectives: 25.3 us -> none  [apply_tilde(): coarse_values = lax.all_gather(slab_values, 'grp', axis=1, tiled=True)]
    all_to_all x6 -> x0, starting transfers between devices: 23.1 us -> none  [the longest x5 16.8 us: partner(): lax.all_to_all(outgoing, 'sub', split_axis=1, concat_axis=1, tiled=True)]
    ppermute x10 -> x0, starting transfers between devices: 21.6 us -> none  [the longest x5 15.2 us: extended(): lax.ppermute(tail, axis, [(i, (i + 1) % count) for i in range(ends)])]
    all_to_all x6 -> x0, waiting for transfers between devices: 15 us -> none  [the longest x5 15 us: partner(): lax.all_to_all(outgoing, 'sub', split_axis=1, concat_axis=1, tiled=True)]
  transfers between devices with their start and end apart: 19 -> 0, of which waited for: 9 -> 0; matrix products, arithmetic and copies ran while one was open for 2% -> 0% of each run, Pallas kernels for 0% -> 0%
where the time goes in v1:
time: 93 us; the launch traced here: 92.5 us
  Pallas kernels  80.4 us (86%)
  local copies, waits for them, and re-layouts  10.7 us (12%)
    pallas_call x1, Pallas kernels, fused_device(): pl.pallas_call(functools.partial(fused_kernel, n_grp, n_sub, peer_rows, c...  80.4 us
    unnamed x19, local copies, waits for them, and re-layouts  9.8 us

profile of v1, /device:TPU:0, one launch (start us, length us, event | category | flops | bytes accessed | tf_op | source)
XLA Modules:
  0.0 92.5 jit_solution(10674985751769775909)
XLA Ops:
  0.6 0.7 copy.15
  1.3 0.7 reduce
  2.0 0.1 reshape_squeeze.3
  2.1 0.1 pad_add_fusion.target_ref
  2.2 0.8 pad.4.cinv_ref
  3.0 0.0 copy-start
  3.0 1.4 %copy-done = bf16[1,1,3,512,512]{4,3,2,1,0:T(8,128)(2,1)S(1)} copy-done((bf16[1,1,3,512,512]{4,3,2,1,0:T(8,128)(2,1)S(1)}, bf16[1,1,3,512,512]{4,3,2,1,0:T(8,128)(2,1)}, u32[]{:S(2)}) %copy-start) | copy-done | bytes 1572888
  4.4 0.0 copy-start.1
  4.4 1.4 %copy-done.1 = bf16[1,1,3,512,512]{4,3,2,1,0:T(8,128)(2,1)S(1)} copy-done((bf16[1,1,3,512,512]{4,3,2,1,0:T(8,128)(2,1)S(1)}, bf16[1,1,3,512,512]{4,3,2,1,0:T(8,128)(2,1)}, u32[]{:S(2)}) %copy-start.1) | copy-done | bytes 1572888
  5.8 0.0 copy-start.2
  5.8 1.0 %copy-done.2 = f32[16,6144]{1,0:T(8,128)S(1)} copy-done((f32[16,6144]{1,0:T(8,128)S(1)}, f32[16,6144]{1,0:T(8,128)}, u32[]{:S(2)}) %copy-start.2) | copy-done | bytes 393240
  6.8 0.0 copy-start.3
  6.8 1.0 %copy-done.3 = bf16[1,1,3,512,128]{4,3,2,1,0:T(8,128)(2,1)S(1)} copy-done((bf16[1,1,3,512,128]{4,3,2,1,0:T(8,128)(2,1)S(1)}, bf16[1,1,3,512,128]{4,3,2,1,0:T(8,128)(2,1)}, u32[]{:S(2)}) %copy-start.3) | copy-done | bytes 393240
  7.8 0.0 copy-start.4
  7.8 0.9 copy-done.4
  8.7 0.0 copy-start.5
  8.7 0.8 copy-done.5
  9.5 0.0 copy-start.6
  9.5 0.7 copy-done.6
  10.1 0.0 copy-start.7
  10.1 0.7 copy-done.7
  10.8 80.4 %shard_map.122 = (f32[16,1536]{1,0:T(8,128)S(1)}, f32[16,1536]{1,0:T(8,128)S(1)}) custom-call(bf16[16,1536]{1,0:T(8,128)(2,1)S(1)} %bitcast.18, f32[16,6144]{1,0:T(8,128)S(1)} %copy-done.2, s32[3,128]{1,0:T(4,128)S(1)} %bitcast.19, bf16[3,512,128]{2,1,0:T(8,128)(2,1)S(1)} %bitcast.14, bf16[3,512,512]{2,1,0:T(8,128)(2,1)S(1)} %bitcast.12, ...), custom_call_target="tpu_custom_call" | custom-call | tf_op jit(solution)/shard_map/pallas_call | solution.py:416
  91.2 0.6 copy.18
  91.9 0.6 copy.19
  (1 shorter events, 0.0 us)
Async XLA Ops:
  3.0 1.4 %copy-start = (bf16[1,1,3,512,512]{4,3,2,1,0:T(8,128)(2,1)S(1)}, bf16[1,1,3,512,512]{4,3,2,1,0:T(8,128)(2,1)}, u32[]{:S(2)}) copy-start(bf16[1,1,3,512,512]{4,3,2,1,0:T(8,128)(2,1)} %param.15) | copy-start | bytes 4718596
  4.4 1.4 %copy-start.1 = (bf16[1,1,3,512,512]{4,3,2,1,0:T(8,128)(2,1)S(1)}, bf16[1,1,3,512,512]{4,3,2,1,0:T(8,128)(2,1)}, u32[]{:S(2)}) copy-start(bf16[1,1,3,512,512]{4,3,2,1,0:T(8,128)(2,1)} %param.16) | copy-start | bytes 4718596
  5.8 1.0 %copy-start.2 = (f32[16,6144]{1,0:T(8,128)S(1)}, f32[16,6144]{1,0:T(8,128)}, u32[]{:S(2)}) copy-start(f32[16,6144]{1,0:T(8,128)} %bound_ref.1) | copy-start | bytes 1179652
  6.8 1.0 %copy-start.3 = (bf16[1,1,3,512,128]{4,3,2,1,0:T(8,128)(2,1)S(1)}, bf16[1,1,3,512,128]{4,3,2,1,0:T(8,128)(2,1)}, u32[]{:S(2)}) copy-start(bf16[1,1,3,512,128]{4,3,2,1,0:T(8,128)(2,1)} %param.14) | copy-start | bytes 1179652
  7.8 0.9 copy-start.4
  8.7 0.8 copy-start.5
  9.5 0.7 copy-start.6
  10.1 0.7 copy-start.7

commit v2 on v1

--- a/solution.py
+++ b/solution.py
@@ -172,10 +172,11 @@
 
 def fused_kernel(
     n_grp, n_sub, peer_rows, coarse,
-    loads_ref, bound_ref, fixed_ref, fixcpl_ref, inv_ref, schur_ref, cpl_ref, target_ref, cinv_ref,
-    counts_ref, slots_ref,
+    loads_hbm, bound_hbm, fixcpl_hbm, inv_hbm, schur_hbm, cpl_hbm, slots_hbm, fixed_ref, target_ref, cinv_ref,
+    counts_ref,
     mult_ref, res_ref,
-    perm, cplf, cplb, cinvf, cinvb, place, ids_all, cinv_all, to_peer, from_peer, to_slab, from_slab,
+    loads_ref, bound_ref, fixcpl_ref, inv_ref, schur_ref, cpl_ref, slots_ref, fetched,
+    perm, perm_t, cplf, cplb, cinvf, cinvb, place, ids_all, cinv_all, to_peer, from_peer, to_slab, from_slab,
     slab_terms, slab_loads,
     id_send, id_recv, cz_send, cz_recv, cg_send, cg_recv,
     p_send, p_recv, h_send, h_recv, t_send, t_recv, l_send, l_recv,
@@ -183,6 +184,14 @@
     g = lax.axis_index("grp")
     s = lax.axis_index("sub")
     length = slots_ref.shape[1]
+    fetch = {}
+    for k, (name, source, held) in enumerate([
+        ("bound", bound_hbm, bound_ref), ("fixcpl", fixcpl_hbm, fixcpl_ref), ("slots", slots_hbm, slots_ref),
+        ("loads", loads_hbm, loads_ref), ("cpl", cpl_hbm, cpl_ref), ("inv", inv_hbm, inv_ref),
+        ("schur", schur_hbm, schur_ref),
+    ]):
+        fetch[name] = pltpu.make_async_copy(source, held, fetched.at[k])
+        fetch[name].start()
     within = n_sub * peer_rows
     corners = SUBS_DEV * CORNERS
     own_rows = coarse // (n_grp * n_sub)
@@ -219,15 +228,44 @@
             copy.start()
         return copies
 
+    mate = g + 1 - 2 * lax.rem(g, 2)
+
+    def coarse_rows_to(k, device, block):
+        return pltpu.make_async_remote_copy(
+            src_ref=cinv_all.at[block], dst_ref=cinv_all.at[block], send_sem=cg_send.at[k], recv_sem=cg_recv.at[k],
+            device_id=(device, s), device_id_type=MESH)
+
+    cz_copies = over_sub(cinv_all.at[g, s], cz_send, cz_recv)
     id_copies = over_sub(ids_all.at[s], id_send, id_recv)
-    cz_copies = over_sub(cinv_all.at[g, s], cz_send, cz_recv)
-
-    chunk = 128
+
+    fetch["bound"].wait()
+    fetch["fixcpl"].wait()
+    bound = bound_ref[...].astype(BF16)
+    lifts = []
+    for a in range(SUBS_DEV):
+        picked = mm(bound, onehot(fixed_ref[a:a + 1, :], 0, bound_ref.shape[1]))
+        lifts.append(mm_nt(picked.astype(BF16), fixcpl_ref[a]))
+    lift = jnp.concatenate(lifts, axis=1)
+
+    for copy in cz_copies:
+        copy.wait()
+    cg_direct = [coarse_rows_to(k, lax.rem(g + k, n_grp), g) for k in range(2, n_grp, 2)]
+    cg_passed = [coarse_rows_to(k + 1, mate, lax.rem(g + n_grp - k, n_grp)) for k in range(0, n_grp, 2)]
+    for copy in cg_direct + cg_passed[:1]:
+        copy.start()
+
+    chunk = LANES
+    fetch["slots"].wait()
 
     @pl.loop(0, length // chunk)
     def _(i):
         start = pl.multiple_of(i * chunk, chunk)
         perm[pl.ds(start, chunk), :] = onehot(slots_ref[...], start, chunk)
+        ids = jnp.broadcast_to(slots_ref[:, pl.ds(start, chunk)].astype(F32), (chunk, chunk))
+        ids = jnp.transpose(ids).astype(jnp.int32)
+        for c in range(length // LANES):
+            at = lax.broadcasted_iota(jnp.int32, (chunk, LANES), 1) + c * LANES
+            perm_t[pl.ds(start, chunk), c * LANES:(c + 1) * LANES] = jnp.where(at == ids, 1.0, 0.0).astype(BF16)
 
     column = lax.broadcasted_iota(jnp.int32, (LOADS, length), 1)
     low = jnp.zeros((LOADS, length), jnp.int32)
@@ -237,28 +275,25 @@
         low = jnp.where(column >= first, first, low)
         count = jnp.where(column >= first, counts_ref[p], count)
     canon_live = jnp.where(column - low < count, 1.0, 0.0).astype(BF16)
-    live = mm_nt(canon_live, perm[...])
-
+    live = mm(canon_live, perm_t[...])
+
+    fetch["cpl"].wait()
     cplf[...] = jnp.zeros_like(cplf)
     for a in range(SUBS_DEV):
         cplf[a * CORNERS:(a + 1) * CORNERS, a * IFACE:(a + 1) * IFACE] = cpl_ref[a].astype(F32)
     cplb[...] = cplf[...].astype(BF16)
 
-    bound = bound_ref[...].astype(BF16)
-    lifts = []
-    for a in range(SUBS_DEV):
-        picked = mm(bound, onehot(fixed_ref[a:a + 1, :], 0, bound_ref.shape[1]))
-        lifts.append(mm_nt(picked.astype(BF16), fixcpl_ref[a]))
-    lifted = live * (loads_ref[...].astype(F32) - jnp.concatenate(lifts, axis=1))
-
-    for copy in cz_copies:
-        copy.wait()
-    cg_copies = over_grp(cinv_all.at[g], cg_send, cg_recv)
+    fetch["loads"].wait()
+    lifted = live * (loads_ref[...].astype(F32) - lift)
+
     for copy in id_copies:
         copy.wait()
     for q in range(n_sub):
         place[:, q * LANES:(q + 1) * LANES] = onehot(ids_all[q], 0, coarse + LANES)
     own_place = onehot(target_ref[...], 0, coarse)
+
+    fetch["inv"].wait()
+    fetch["schur"].wait()
 
     def blocks_apply(ref, field_b):
         return jnp.concatenate(
@@ -288,10 +323,15 @@
         total_high = total.astype(BF16)
         slab_loads[i, g] = jnp.concatenate(
             [dense[:, :coarse].astype(BF16), total_high, (total - total_high.astype(F32)).astype(BF16)], axis=1)
-        for copy in over_grp(slab_loads.at[i, g], l_send.at[i], l_recv.at[i]):
+        load_copies = over_grp(slab_loads.at[i, g], l_send.at[i], l_recv.at[i])
+        if i == 0:
+            for copy, passed in zip(cg_direct, cg_passed[1:]):
+                copy.wait()
+                passed.start()
+        for copy in load_copies:
             copy.wait()
         if i == 0:
-            for copy in cg_copies:
+            for copy in cg_passed:
                 copy.wait()
             for d in range(n_grp * n_sub):
                 part = cinv_all[d // n_sub, d % n_sub].astype(F32)
@@ -352,7 +392,7 @@
 
         joined = jnp.concatenate(
             [from_peer[i, q] for q in range(n_sub)] + [from_slab[i, q] for q in range(2)], axis=1)
-        return mm_nt(joined, perm[...])
+        return mm(joined, perm_t[...])
 
     def smoothed(residual):
         return blocks_apply(schur_ref, residual.astype(BF16))
@@ -409,16 +449,23 @@
     held = -(-rows // 16) * 16
     coarse_rows = jnp.pad(coarse_inverse, ((0, held - rows), (0, 0)))
     vmem = pl.BlockSpec(memory_space=pltpu.VMEM)
+    hbm = pl.BlockSpec(memory_space=pltpu.HBM)
     smem = pl.BlockSpec(memory_space=pltpu.SMEM)
     swaps, solves = 2 * ITERS + 1, ITERS + 1
     dma = pltpu.SemaphoreType.DMA
     field = jax.ShapeDtypeStruct((LOADS, length), F32)
+    fetched = (
+        loads[0, 0], boundary_values, dirichlet_coupling[0, 0], local_inverse[0, 0], local_schur[0, 0],
+        corner_coupling[0, 0], slot_of[0],
+    )
     mult, res = pl.pallas_call(
         functools.partial(fused_kernel, n_grp, n_sub, peer_rows, coarse),
         out_shape=(field, field),
-        in_specs=[vmem] * 9 + [smem, vmem],
+        in_specs=[hbm] * 7 + [vmem] * 3 + [smem],
         out_specs=(vmem, vmem),
-        scratch_shapes=[
+        scratch_shapes=[pltpu.VMEM(x.shape, x.dtype) for x in fetched] + [
+            dma((len(fetched),)),
+            pltpu.VMEM((length, length), BF16),
             pltpu.VMEM((length, length), BF16),
             pltpu.VMEM((LANES, length), F32),
             pltpu.VMEM((LANES, length), BF16),
@@ -439,10 +486,7 @@
         ],
         compiler_params=pltpu.CompilerParams(
             collective_id=0, has_side_effects=True, vmem_limit_bytes=48 << 20),
-    )(
-        loads[0, 0], boundary_values, dirichlet_ids[0, 0], dirichlet_coupling[0, 0], local_inverse[0, 0],
-        local_schur[0, 0], corner_coupling[0, 0], target, coarse_rows, row_counts[0, 0], slot_of[0],
-    )
+    )(*fetched, dirichlet_ids[0, 0], target, coarse_rows, row_counts[0, 0])
     return (mult[None, None], res[None, None])
 
 
@@ -451,6 +495,7 @@
     peer_rows = (args[10].shape[2] - 2 * SLAB_ROWS) // lax.axis_size("sub")
     small = coarse * coarse * args[8].dtype.itemsize <= WHOLE_COARSE_BYTES
     aligned = peer_rows % LANES == 0 and coarse % LANES == 0 and args[8].shape[0] % 8 == 0
+    aligned = aligned and lax.axis_size("grp") % 2 == 0
     return (fused_device if small and aligned else spread_device)(*args)
 
 

time: 93 us -> 82.9 us (0.89)
  Pallas kernels: 80.4 us -> 70.3 us
    pallas_call x1, Pallas kernels: 80.4 us -> 70.3 us  [fused_device(): pl.pallas_call(functools.partial(fused_kernel, n_grp, n_sub, peer_rows, c...]
where the time goes in v2:
time: 82.9 us; the launch traced here: 82.4 us
  Pallas kernels  70.3 us (85%)
  local copies, waits for them, and re-layouts  10.7 us (13%)
    pallas_call x1, Pallas kernels, fused_device(): pl.pallas_call(functools.partial(fused_kernel, n_grp, n_sub, peer_rows, c...  70.3 us
    unnamed x19, local copies, waits for them, and re-layouts  9.8 us

profile of v2, /device:TPU:0, one launch (start us, length us, event | category | flops | bytes accessed | tf_op | source)
XLA Modules:
  0.0 82.4 jit_solution(15794500275667860286)
XLA Ops:
  0.6 0.7 copy.15
  1.3 0.7 reduce
  2.0 0.1 reshape_squeeze.3
  2.1 0.1 pad_add_fusion.target_ref
  2.2 0.8 pad.4.cinv_ref
  3.0 0.0 copy-start
  3.0 1.4 %copy-done = bf16[1,1,3,512,512]{4,3,2,1,0:T(8,128)(2,1)S(1)} copy-done((bf16[1,1,3,512,512]{4,3,2,1,0:T(8,128)(2,1)S(1)}, bf16[1,1,3,512,512]{4,3,2,1,0:T(8,128)(2,1)}, u32[]{:S(2)}) %copy-start) | copy-done | bytes 1572888
  4.4 0.0 copy-start.1
  4.4 1.4 %copy-done.1 = bf16[1,1,3,512,512]{4,3,2,1,0:T(8,128)(2,1)S(1)} copy-done((bf16[1,1,3,512,512]{4,3,2,1,0:T(8,128)(2,1)S(1)}, bf16[1,1,3,512,512]{4,3,2,1,0:T(8,128)(2,1)}, u32[]{:S(2)}) %copy-start.1) | copy-done | bytes 1572888
  5.8 0.0 copy-start.2
  5.8 1.0 %copy-done.2 = f32[16,6144]{1,0:T(8,128)S(1)} copy-done((f32[16,6144]{1,0:T(8,128)S(1)}, f32[16,6144]{1,0:T(8,128)}, u32[]{:S(2)}) %copy-start.2) | copy-done | bytes 393240
  6.8 0.0 copy-start.3
  6.8 1.0 %copy-done.3 = bf16[1,1,3,512,128]{4,3,2,1,0:T(8,128)(2,1)S(1)} copy-done((bf16[1,1,3,512,128]{4,3,2,1,0:T(8,128)(2,1)S(1)}, bf16[1,1,3,512,128]{4,3,2,1,0:T(8,128)(2,1)}, u32[]{:S(2)}) %copy-start.3) | copy-done | bytes 393240
  7.8 0.0 copy-start.4
  7.8 0.9 %copy-done.4 = bf16[1,1,3,24,512]{4,3,2,1,0:T(8,128)(2,1)S(1)} copy-done((bf16[1,1,3,24,512]{4,3,2,1,0:T(8,128)(2,1)S(1)}, bf16[1,1,3,24,512]{4,3,2,1,0:T(8,128)(2,1)}, u32[]{:S(2)}) %copy-start.4) | copy-done | bytes 73752
  8.7 0.0 copy-start.5
  8.7 0.8 copy-done.5
  9.5 0.0 copy-start.6
  9.5 0.7 copy-done.6
  10.1 0.0 copy-start.7
  10.1 0.7 copy-done.7
  10.8 70.3 %shard_map.122 = (f32[16,1536]{1,0:T(8,128)S(1)}, f32[16,1536]{1,0:T(8,128)S(1)}) custom-call(bf16[16,1536]{1,0:T(8,128)(2,1)S(1)} %bitcast.18, f32[16,6144]{1,0:T(8,128)S(1)} %copy-done.2, bf16[3,512,128]{2,1,0:T(8,128)(2,1)S(1)} %bitcast.14, bf16[3,512,512]{2,1,0:T(8,128)(2,1)S(1)} %bitcast.12, bf16[3,512,512]{2,1,0:T(8,128)(2,1)S(1)} %bitcast.13, ...), custom_call_target="tpu_custom_call" | custom-call | tf_op jit(solution)/shard_map/pallas_call | solution.py:461
  81.1 0.6 copy.18
  81.8 0.6 copy.19
  (1 shorter events, 0.0 us)
Async XLA Ops:
  3.0 1.4 %copy-start = (bf16[1,1,3,512,512]{4,3,2,1,0:T(8,128)(2,1)S(1)}, bf16[1,1,3,512,512]{4,3,2,1,0:T(8,128)(2,1)}, u32[]{:S(2)}) copy-start(bf16[1,1,3,512,512]{4,3,2,1,0:T(8,128)(2,1)} %param.15) | copy-start | bytes 4718596
  4.4 1.4 %copy-start.1 = (bf16[1,1,3,512,512]{4,3,2,1,0:T(8,128)(2,1)S(1)}, bf16[1,1,3,512,512]{4,3,2,1,0:T(8,128)(2,1)}, u32[]{:S(2)}) copy-start(bf16[1,1,3,512,512]{4,3,2,1,0:T(8,128)(2,1)} %param.16) | copy-start | bytes 4718596
  5.8 1.0 %copy-start.2 = (f32[16,6144]{1,0:T(8,128)S(1)}, f32[16,6144]{1,0:T(8,128)}, u32[]{:S(2)}) copy-start(f32[16,6144]{1,0:T(8,128)} %bound_hbm.1) | copy-start | bytes 1179652
  6.8 1.0 %copy-start.3 = (bf16[1,1,3,512,128]{4,3,2,1,0:T(8,128)(2,1)S(1)}, bf16[1,1,3,512,128]{4,3,2,1,0:T(8,128)(2,1)}, u32[]{:S(2)}) copy-start(bf16[1,1,3,512,128]{4,3,2,1,0:T(8,128)(2,1)} %param.14) | copy-start | bytes 1179652
  7.8 0.9 %copy-start.4 = (bf16[1,1,3,24,512]{4,3,2,1,0:T(8,128)(2,1)S(1)}, bf16[1,1,3,24,512]{4,3,2,1,0:T(8,128)(2,1)}, u32[]{:S(2)}) copy-start(bf16[1,1,3,24,512]{4,3,2,1,0:T(8,128)(2,1)} %param.17) | copy-start | bytes 221188
  8.7 0.8 copy-start.5
  9.5 0.7 copy-start.6
  10.1 0.7 copy-start.7

commit v3 on v2

--- a/solution.py
+++ b/solution.py
@@ -260,7 +260,6 @@
     @pl.loop(0, length // chunk)
     def _(i):
         start = pl.multiple_of(i * chunk, chunk)
-        perm[pl.ds(start, chunk), :] = onehot(slots_ref[...], start, chunk)
         ids = jnp.broadcast_to(slots_ref[:, pl.ds(start, chunk)].astype(F32), (chunk, chunk))
         ids = jnp.transpose(ids).astype(jnp.int32)
         for c in range(length // LANES):
@@ -286,10 +285,17 @@
     fetch["loads"].wait()
     lifted = live * (loads_ref[...].astype(F32) - lift)
 
-    for copy in id_copies:
-        copy.wait()
-    for q in range(n_sub):
-        place[:, q * LANES:(q + 1) * LANES] = onehot(ids_all[q], 0, coarse + LANES)
+    def late_tables():
+        for copy in id_copies:
+            copy.wait()
+        for q in range(n_sub):
+            place[:, q * LANES:(q + 1) * LANES] = onehot(ids_all[q], 0, coarse + LANES)
+
+        @pl.loop(0, length // chunk)
+        def _(i):
+            start = pl.multiple_of(i * chunk, chunk)
+            perm[pl.ds(start, chunk), :] = onehot(slots_ref[...], start, chunk)
+
     own_place = onehot(target_ref[...], 0, coarse)
 
     fetch["inv"].wait()
@@ -307,12 +313,16 @@
     def tilde(i, field, extra):
         field_b = field.astype(BF16)
         message = mm_nt(field_b, cplb[...])
-        local = blocks_apply(inv_ref, field_b)
+        local = blocks_apply(inv_ref, field_b) if i > 0 else None
         sums = extra(local)
         for k, part in enumerate(sums):
             message = jnp.where(lane == corners + k, part, message)
         slab_terms[i, s] = message
-        for copy in over_sub(slab_terms.at[i, s], t_send.at[i], t_recv.at[i]):
+        term_copies = over_sub(slab_terms.at[i, s], t_send.at[i], t_recv.at[i])
+        if i == 0:
+            local = blocks_apply(inv_ref, field_b)
+            late_tables()
+        for copy in term_copies:
             copy.wait()
         terms = jnp.concatenate([slab_terms[i, q] for q in range(n_sub)], axis=1)
         high = terms.astype(BF16)

time: 82.9 us -> 82.6 us (level)
  no operation moved by 1% of the time
where the time goes in v3:
time: 82.6 us; the launch traced here: 82.1 us
  Pallas kernels  70 us (85%)
  local copies, waits for them, and re-layouts  10.7 us (13%)
    pallas_call x1, Pallas kernels, fused_device(): pl.pallas_call(functools.partial(fused_kernel, n_grp, n_sub, peer_rows, c...  70 us
    unnamed x19, local copies, waits for them, and re-layouts  9.8 us

profile of v3, /device:TPU:0, one launch (start us, length us, event | category | flops | bytes accessed | tf_op | source)
XLA Modules:
  0.0 82.1 jit_solution(4978096267454012230)
XLA Ops:
  0.6 0.7 copy.15
  1.3 0.7 reduce
  2.0 0.1 reshape_squeeze.3
  2.1 0.1 pad_add_fusion.target_ref
  2.2 0.8 pad.4.cinv_ref
  3.0 0.0 copy-start
  3.0 1.4 %copy-done = bf16[1,1,3,512,512]{4,3,2,1,0:T(8,128)(2,1)S(1)} copy-done((bf16[1,1,3,512,512]{4,3,2,1,0:T(8,128)(2,1)S(1)}, bf16[1,1,3,512,512]{4,3,2,1,0:T(8,128)(2,1)}, u32[]{:S(2)}) %copy-start) | copy-done | bytes 1572888
  4.4 0.0 copy-start.1
  4.4 1.4 %copy-done.1 = bf16[1,1,3,512,512]{4,3,2,1,0:T(8,128)(2,1)S(1)} copy-done((bf16[1,1,3,512,512]{4,3,2,1,0:T(8,128)(2,1)S(1)}, bf16[1,1,3,512,512]{4,3,2,1,0:T(8,128)(2,1)}, u32[]{:S(2)}) %copy-start.1) | copy-done | bytes 1572888
  5.8 0.0 copy-start.2
  5.8 1.0 %copy-done.2 = f32[16,6144]{1,0:T(8,128)S(1)} copy-done((f32[16,6144]{1,0:T(8,128)S(1)}, f32[16,6144]{1,0:T(8,128)}, u32[]{:S(2)}) %copy-start.2) | copy-done | bytes 393240
  6.8 0.0 copy-start.3
  6.8 1.0 %copy-done.3 = bf16[1,1,3,512,128]{4,3,2,1,0:T(8,128)(2,1)S(1)} copy-done((bf16[1,1,3,512,128]{4,3,2,1,0:T(8,128)(2,1)S(1)}, bf16[1,1,3,512,128]{4,3,2,1,0:T(8,128)(2,1)}, u32[]{:S(2)}) %copy-start.3) | copy-done | bytes 393240
  7.8 0.0 copy-start.4
  7.8 0.9 %copy-done.4 = bf16[1,1,3,24,512]{4,3,2,1,0:T(8,128)(2,1)S(1)} copy-done((bf16[1,1,3,24,512]{4,3,2,1,0:T(8,128)(2,1)S(1)}, bf16[1,1,3,24,512]{4,3,2,1,0:T(8,128)(2,1)}, u32[]{:S(2)}) %copy-start.4) | copy-done | bytes 73752
  8.7 0.0 copy-start.5
  8.7 0.8 copy-done.5
  9.5 0.0 copy-start.6
  9.5 0.7 copy-done.6
  10.1 0.0 copy-start.7
  10.1 0.7 copy-done.7
  10.8 70.0 %shard_map.122 = (f32[16,1536]{1,0:T(8,128)S(1)}, f32[16,1536]{1,0:T(8,128)S(1)}) custom-call(bf16[16,1536]{1,0:T(8,128)(2,1)S(1)} %bitcast.18, f32[16,6144]{1,0:T(8,128)S(1)} %copy-done.2, bf16[3,512,128]{2,1,0:T(8,128)(2,1)S(1)} %bitcast.14, bf16[3,512,512]{2,1,0:T(8,128)(2,1)S(1)} %bitcast.12, bf16[3,512,512]{2,1,0:T(8,128)(2,1)S(1)} %bitcast.13, ...), custom_call_target="tpu_custom_call" | custom-call | tf_op jit(solution)/shard_map/pallas_call | solution.py:471
  80.8 0.6 copy.18
  81.5 0.6 copy.19
  (1 shorter events, 0.0 us)
Async XLA Ops:
  3.0 1.4 %copy-start = (bf16[1,1,3,512,512]{4,3,2,1,0:T(8,128)(2,1)S(1)}, bf16[1,1,3,512,512]{4,3,2,1,0:T(8,128)(2,1)}, u32[]{:S(2)}) copy-start(bf16[1,1,3,512,512]{4,3,2,1,0:T(8,128)(2,1)} %param.15) | copy-start | bytes 4718596
  4.4 1.4 %copy-start.1 = (bf16[1,1,3,512,512]{4,3,2,1,0:T(8,128)(2,1)S(1)}, bf16[1,1,3,512,512]{4,3,2,1,0:T(8,128)(2,1)}, u32[]{:S(2)}) copy-start(bf16[1,1,3,512,512]{4,3,2,1,0:T(8,128)(2,1)} %param.16) | copy-start | bytes 4718596
  5.8 1.0 %copy-start.2 = (f32[16,6144]{1,0:T(8,128)S(1)}, f32[16,6144]{1,0:T(8,128)}, u32[]{:S(2)}) copy-start(f32[16,6144]{1,0:T(8,128)} %bound_hbm.1) | copy-start | bytes 1179652
  6.8 1.0 %copy-start.3 = (bf16[1,1,3,512,128]{4,3,2,1,0:T(8,128)(2,1)S(1)}, bf16[1,1,3,512,128]{4,3,2,1,0:T(8,128)(2,1)}, u32[]{:S(2)}) copy-start(bf16[1,1,3,512,128]{4,3,2,1,0:T(8,128)(2,1)} %param.14) | copy-start | bytes 1179652
  7.8 0.9 %copy-start.4 = (bf16[1,1,3,24,512]{4,3,2,1,0:T(8,128)(2,1)S(1)}, bf16[1,1,3,24,512]{4,3,2,1,0:T(8,128)(2,1)}, u32[]{:S(2)}) copy-start(bf16[1,1,3,24,512]{4,3,2,1,0:T(8,128)(2,1)} %param.17) | copy-start | bytes 221188
  8.7 0.8 copy-start.5
  9.5 0.7 copy-start.6
  10.1 0.7 copy-start.7
